TPU v7x, 32 devices: a whole 2x2x4 slice. The times are simulated.
32 devices in a mesh: wide: 8 (over z, y), narrow: 4 (over x, core).
Axes of the slice: x: 2, y: 2, z: 4, core: 2. Of those that a mesh axis runs over, the one named last changes fastest.
Arguments:
- a_blocks: bfloat16 [6144, 64, 512], P(('wide', 'narrow')), may hold values from -0.25 to 0.25
- a_columns: int32 [6144, 8], P(('wide', 'narrow')), may hold values from 0 to 6143, as said below
- p_blocks: bfloat16 [6144, 64, 192], P(('wide', 'narrow')), may hold values from -0.75 to 0.75
- p_pattern: int32 [6144, 3], P(('wide', 'narrow')), may hold values from 0 to 1, as said below
- aggregate: int32 [6144], P(('wide', 'narrow')), may hold values from 0 to 63, as said below
- owner_map: int32 [64], replicated, may hold values from 0 to 31, as said below
Outputs:
- owned_coarse: bfloat16 [256, 64, 192], P(('wide', 'narrow'))
Inputs may be any that keep to these rules, and one draw needn't show every extreme that they name: `a_columns`: entry 0 of row i is i; every entry lies within 32 rows of i; entries 1 and 2 are i - 32 and i + 32, clipped to 0 to 6143. `aggregate`: Non-decreasing; the aligned block of rows g * 192 to (g + 1) * 192 - 1 holds exactly aggregates g * 2 to (g + 1) * 2 - 1, each a run of 48 rows or more. `p_pattern`: entry 1 is always 1; entry 0 can be 1 only on the first 8 rows of an aggregate other than aggregate 0, entry 2 only on the last 8 rows of an aggregate other than the last one. `owner_map`: with N devices, N / 8 devices own exactly 8 aggregates each, N - N / 2 devices own exactly 2 each, and the others none; which devices is drawn.
All inputs are finite; a program needn't handle non-finite values.
Results may differ from a plain program's by a relative error of at most 0.005.
Values may be sent and summed in bfloat16 or wider, within the bound.
A program may use at most 128 MiB of HBM per device.

v0:
```python
import functools

import jax
import jax.numpy as jnp
from jax import lax
from jax.experimental import pallas as pl
from jax.experimental.pallas import tpu as pltpu
from jax.sharding import PartitionSpec as P

HR = 32
LW = 2
OWNMAX = 8
GROUP = 8
SPR = 8
AXES = ("wide", "narrow")


def kernel(a_hbm, cols, p_hbm, pattern, aggregate, g_ref,
           a_v, p_v, pooled, applied, packed, rim, rim_side, a_sem, p_sem, send_sem, recv_sem):
    rows, nodes = a_hbm.shape[0], a_hbm.shape[1]
    me = lax.axis_index(AXES)
    groups = rows // GROUP
    shift = HR // GROUP
    first_inner = (HR + SPR) // GROUP
    narrow = lax.axis_size("narrow")
    count = lax.axis_size(AXES)
    mesh_id = pl.DeviceIdType.MESH
    others = [lax.rem(me + 1, count), lax.rem(me + count - 1, count)]
    others = [(other // narrow, lax.rem(other, narrow)) for other in others]
    barrier = pltpu.get_barrier_semaphore()
    for other in others:
        pl.semaphore_signal(barrier, inc=1, device_id=other, device_id_type=mesh_id)

    def p_copy(g):
        span = pl.ds(g * GROUP, GROUP)
        return pltpu.make_async_copy(p_hbm.at[span], p_v.at[span], p_sem.at[g])

    def a_copy(g):
        span = pl.ds(g * GROUP, GROUP)
        return pltpu.make_async_copy(a_hbm.at[span], a_v.at[span], a_sem.at[g])

    @pl.loop(0, groups)
    def _(step):
        p_copy(lax.rem(step + groups - shift, groups)).start()

    @pl.loop(0, groups)
    def _(g):
        a_copy(lax.rem(g + first_inner, groups)).start()

    left = lax.broadcasted_iota(jnp.int32, (nodes, 128), 1) < 64

    def place_group(step, at_end):
        g = lax.rem(step + groups - shift, groups)
        p_copy(g).wait()
        for j in range(GROUP):
            i = g * GROUP + j
            second = aggregate[i] - me * LW == 1
            has0 = pattern[i, 0] == 1
            has2 = pattern[i, 2] == 1
            x0 = p_v[i, :, :128]
            x2 = p_v[i, :, 128:]
            swapped = jnp.concatenate([x0[:, 64:], x0[:, :64]], axis=1)
            twice = jnp.concatenate([x2, x2], axis=1)
            bit = lambda flag: jnp.where(flag, 1.0, 0.0).astype(jnp.bfloat16)
            one = jnp.ones_like(x0)
            first_low = jnp.where(left, swapped, twice * bit(has2))
            second_low = x0 * jnp.where(left, one * bit(has0), one)
            pooled[HR + i, :, :128] = first_low * bit(~second) + second_low * bit(second)
            if at_end:
                pooled[HR + i, :, 128:] = jnp.where(
                    left, twice * bit(has2 & second), swapped * bit(has0 & ~second)
                )
            else:
                pooled[HR + i, :, 128:] = jnp.zeros_like(x0)

    def rim_copies(side):
        end = pl.ds(rows + HR - SPR if side == 0 else HR, SPR)
        pairs = (
            (packed.at[side], rim.at[side]),
            (pooled.at[end, :, pl.ds(128, 128)], rim_side.at[side]),
        )
        return [
            pltpu.make_async_remote_copy(
                src_ref=source,
                dst_ref=landing,
                send_sem=send_sem.at[side, half],
                recv_sem=recv_sem.at[side, half],
                device_id=others[side],
                device_id_type=mesh_id,
            )
            for half, (source, landing) in enumerate(pairs)
        ]

    pl.loop(0, 2 * shift)(functools.partial(place_group, at_end=True))

    @pl.loop(0, HR // 2)
    def _(i):
        for side, first, at in ((0, rows, 64), (1, HR, 0)):
            packed[side, i] = jnp.concatenate(
                [pooled[first + i + k, :, at : at + 64] for k in (0, HR // 2)], axis=1
            )

    pl.semaphore_wait(barrier, 2)
    copies = rim_copies(0) + rim_copies(1)
    for copy in copies:
        copy.start()
    pl.loop(2 * shift, groups)(functools.partial(place_group, at_end=False))

    g_ref[...] = jnp.zeros_like(g_ref)
    base = HR - me * rows
    limit = pooled.shape[0] - 1

    def transposed_product(span_rows, lanes, width):
        left_rows = pooled[span_rows, :, lanes].reshape(GROUP * nodes, 128)
        return lax.dot_general(
            left_rows, applied[:, :width], (((0,), (0,)), ((), ())), preferred_element_type=jnp.float32
        )

    def run_group(step, width):
        g = lax.rem(step + first_inner, groups)
        a_copy(g).wait()
        for j in range(GROUP):
            i = g * GROUP + j
            total = None
            for h in range(2):
                stack = jnp.concatenate(
                    [
                        pooled[jnp.clip(cols[i, 4 * h + k] + base, 0, limit), :, :width]
                        for k in range(4)
                    ],
                    axis=0,
                )
                part = jnp.dot(
                    a_v[i, :, 256 * h : 256 * (h + 1)], stack, preferred_element_type=jnp.float32
                )
                total = part if total is None else total + part
            applied[j * nodes : (j + 1) * nodes, :width] = total.astype(jnp.bfloat16)
        span = pl.ds(HR + g * GROUP, GROUP)
        g_ref[:128, :width] += transposed_product(span, pl.ds(0, 128), width)
        if width == 128:
            return

        @pl.when((g == 0) | (g == groups - 1))
        def _():
            g_ref[128:, :] += transposed_product(span, pl.ds(128, 128), width)

    inner = groups - 2 * first_inner
    pl.loop(0, inner)(functools.partial(run_group, width=128))
    for copy in copies:
        copy.wait()

    @pl.loop(0, HR // 2)
    def _(i):
        blank = jnp.zeros((nodes, 64), jnp.bfloat16)
        for side, first in enumerate((0, rows + HR)):
            for k in range(2):
                row = first + i + k * (HR // 2)
                own = rim[side, i, :, 64 * k : 64 * (k + 1)]
                pooled[row, :, :128] = jnp.zeros((nodes, 128), jnp.bfloat16)
                pooled[row, :, 128:] = jnp.concatenate(
                    [blank, own] if side == 0 else [own, blank], axis=1
                )

    @pl.loop(0, SPR)
    def _(i):
        for side, first in enumerate((HR - SPR, rows + HR)):
            pooled[first + i, :, :128] = rim_side[side, i]

    pl.loop(inner, groups)(functools.partial(run_group, width=256))


def gather_kernel(wide, narrow, total, owner_map, out, edge_out, edge_in, every,
                  edge_send, edge_recv, send_sem, recv_sem):
    w, n = lax.axis_index("wide"), lax.axis_index("narrow")
    me = w * narrow + n
    nodes = out.shape[1]
    count = wide * narrow
    following, preceding = lax.rem(me + 1, count), lax.rem(me + count - 1, count)
    beside = n + 1 - 2 * lax.rem(n, 2)
    across = lax.rem(n + 2, 4)
    mesh_id = pl.DeviceIdType.MESH

    barrier = pltpu.get_barrier_semaphore()
    for other in (following, preceding):
        pl.semaphore_signal(
            barrier, inc=1, device_id=(other // narrow, lax.rem(other, narrow)), device_id_type=mesh_id
        )
    for other in (beside, across):
        pl.semaphore_signal(barrier, inc=1, device_id=(w, other), device_id_type=mesh_id)

    def greet(d, carry):
        pl.semaphore_signal(
            barrier, inc=1, device_id=(lax.rem(w + d, wide), n), device_id_type=mesh_id
        )
        return carry

    lax.fori_loop(1, wide, greet, 0)

    edge_out[0] = total[2 * nodes : 3 * nodes, nodes : 3 * nodes]
    edge_out[1] = jnp.concatenate(
        [total[3 * nodes :, 3 * nodes :], total[3 * nodes :, :nodes]], axis=1
    )
    pl.semaphore_wait(barrier, wide + 3)

    def edge_copy(side, other):
        return pltpu.make_async_remote_copy(
            src_ref=edge_out.at[side],
            dst_ref=edge_in.at[side],
            send_sem=edge_send.at[side],
            recv_sem=edge_recv.at[side],
            device_id=(other // narrow, lax.rem(other, narrow)),
            device_id_type=mesh_id,
        )

    edges = [edge_copy(0, following), edge_copy(1, preceding)]
    for edge in edges:
        edge.start()
    def visit(a, found):
        hit = owner_map[a] == me
        rank = found[0]
        spots = tuple(
            jnp.where(hit & (rank == s), a, spot) for s, spot in enumerate(found[1:])
        )
        return (rank + jnp.where(hit, 1, 0),) + spots

    found = lax.fori_loop(
        0, owner_map.shape[0], visit, (jnp.int32(0),) + (jnp.int32(0),) * OWNMAX
    )

    for edge in edges:
        edge.wait()

    def store(slot, which, front, tail):
        every[slot, which, :64, :] = front.astype(jnp.bfloat16)
        tail = tail.astype(jnp.bfloat16)
        every[slot, which, 64:, :] = jnp.concatenate([tail[:32], tail[32:]], axis=1)

    own = jnp.concatenate([total[:nodes, 3 * nodes :], total[:nodes, :nodes]], axis=1)
    store(me, 0, own + edge_in[0], total[:nodes, nodes : 2 * nodes])
    own = total[nodes : 2 * nodes, : 2 * nodes]
    extra = edge_in[1]
    moved = jnp.concatenate([jnp.zeros_like(extra[:, :nodes]), extra[:, :nodes]], axis=1)
    last = total[nodes : 2 * nodes, 2 * nodes : 3 * nodes] + extra[:, nodes:]
    store(me, 1, own + moved, last)

    def copy(kind, d, slot, device):
        return pltpu.make_async_remote_copy(
            src_ref=every.at[slot],
            dst_ref=every.at[slot],
            send_sem=send_sem.at[kind, d],
            recv_sem=recv_sem.at[slot],
            device_id=device,
            device_id_type=mesh_id,
        )

    def along(d):
        return copy(0, d, me, (lax.rem(w + d, wide), n))

    def forward(d):
        slot = lax.rem(w + wide - d, wide) * narrow + n
        return copy(1, d, slot, (w, across)), copy(2, d, slot, (w, beside))

    def relay(d):
        slot = lax.rem(w + wide - d, wide) * narrow + across
        return copy(3, d, slot, (w, beside))

    def slot_at(d, column):
        return lax.rem(w + wide - d, wide) * narrow + column

    def send_along(d, carry):
        along(d).start()
        return carry

    lax.fori_loop(1, wide, send_along, 0)

    def pass_on(d, carry):
        @pl.when(d > 0)
        def _():
            copy(0, d, slot_at(d, n), (w, across)).wait_recv()

        for c in forward(d):
            c.start()
        return carry

    lax.fori_loop(0, wide, pass_on, 0)

    def pass_second(d, carry):
        copy(1, d, slot_at(d, across), (w, across)).wait_recv()
        relay(d).start()
        return carry

    lax.fori_loop(0, wide, pass_second, 0)

    across_beside = lax.rem(beside + 2, 4)

    def finish(d, carry):
        copy(2, d, slot_at(d, beside), (w, beside)).wait_recv()
        copy(3, d, slot_at(d, across_beside), (w, beside)).wait_recv()
        for c in forward(d):
            c.wait_send()
        relay(d).wait_send()

        @pl.when(d > 0)
        def _():
            along(d).wait_send()

        return carry

    lax.fori_loop(0, wide, finish, 0)

    for s in range(OWNMAX):
        spot = found[1 + s]
        keep = jnp.where(s < found[0], 1.0, 0.0)
        row = every[spot // LW, lax.rem(spot, LW)].astype(jnp.float32) * keep
        row = row.astype(jnp.bfloat16)
        out[s, :, :128] = row[:64]
        out[s, :32, 128:] = row[64:, :64]
        out[s, 32:, 128:] = row[64:, 64:]


def shards(a_blocks, a_columns, p_blocks, p_pattern, aggregate, owner_map):
    rows, nodes = a_blocks.shape[:2]
    count = lax.axis_size(AXES)
    vmem = pl.BlockSpec(memory_space=pltpu.VMEM)
    smem = pl.BlockSpec(memory_space=pltpu.SMEM)
    hbm = pl.BlockSpec(memory_space=pl.ANY)
    groups = rows // GROUP
    total = pl.pallas_call(
        kernel,
        out_shape=jax.ShapeDtypeStruct((4 * nodes, 4 * nodes), jnp.float32),
        in_specs=[hbm, smem, hbm, smem, smem],
        out_specs=vmem,
        scratch_shapes=[
            pltpu.VMEM(a_blocks.shape, jnp.bfloat16),
            pltpu.VMEM(p_blocks.shape, jnp.bfloat16),
            pltpu.VMEM((rows + 2 * HR, nodes, 4 * nodes), jnp.bfloat16),
            pltpu.VMEM((GROUP * nodes, 4 * nodes), jnp.bfloat16),
            pltpu.VMEM((2, HR // 2, nodes, 2 * nodes), jnp.bfloat16),
            pltpu.VMEM((2, HR // 2, nodes, 2 * nodes), jnp.bfloat16),
            pltpu.VMEM((2, SPR, nodes, 2 * nodes), jnp.bfloat16),
            pltpu.SemaphoreType.DMA((groups,)),
            pltpu.SemaphoreType.DMA((groups,)),
            pltpu.SemaphoreType.DMA((2, 2)),
            pltpu.SemaphoreType.DMA((2, 2)),
        ],
        compiler_params=pltpu.CompilerParams(
            collective_id=1, has_side_effects=True, vmem_limit_bytes=48 << 20
        ),
    )(a_blocks, a_columns, p_blocks, p_pattern, aggregate)
    wide, narrow = lax.axis_size("wide"), lax.axis_size("narrow")
    return pl.pallas_call(
        functools.partial(gather_kernel, wide, narrow),
        out_shape=jax.ShapeDtypeStruct((OWNMAX, nodes, 3 * nodes), jnp.bfloat16),
        in_specs=[vmem, smem],
        out_specs=vmem,
        scratch_shapes=[
            pltpu.VMEM((2, nodes, 2 * nodes), jnp.float32),
            pltpu.VMEM((2, nodes, 2 * nodes), jnp.float32),
            pltpu.VMEM((count, LW, 96, 128), jnp.bfloat16),
            pltpu.SemaphoreType.DMA((2,)),
            pltpu.SemaphoreType.DMA((2,)),
            pltpu.SemaphoreType.DMA((4, wide)),
            pltpu.SemaphoreType.DMA((count,)),
        ],
        compiler_params=pltpu.CompilerParams(
            collective_id=0, has_side_effects=True, vmem_limit_bytes=32 << 20
        ),
    )(total, owner_map)


def solution(mesh):
    placed = (
        P(AXES, None, None),
        P(AXES, None),
        P(AXES, None, None),
        P(AXES, None),
        P(AXES),
        P(),
    )
    return jax.shard_map(
        shards,
        mesh=mesh,
        in_specs=placed,
        out_specs=P(AXES, None, None),
        check_vma=False,
    )
```

profile of v0, /device:TPU:0, one launch (start us, length us, event | category | flops | bytes accessed | tf_op | source)
XLA Modules:
  0.0 55.1 jit_solution(14363053881221562611)
XLA Ops:
  0.0 0.0 copy-start.1
  0.0 0.8 %copy.7.cols = s32[192,8]{1,0:T(8,128)S(1)} copy(s32[192,8]{0,1:T(8,128)} %param.7) | data formatting | bytes 12288 | tf_op args[1]
  0.8 0.8 %copy.8.pattern = s32[192,3]{1,0:T(8,128)S(1)} copy(s32[192,3]{0,1:T(4,128)} %param.9) | data formatting | bytes 4608 | tf_op args[3]
  1.6 0.0 copy-start
  1.6 0.7 %copy-done = s32[192]{0:T(256)S(1)} copy-done((s32[192]{0:T(256)S(1)}, s32[192]{0:T(256)}, u32[]{:S(2)}) %copy-start) | copy-done | bytes 792
  2.3 29.7 %shard_map.64.total = f32[256,256]{1,0:T(8,128)S(1)} custom-call(bf16[192,64,512]{2,1,0:T(8,128)(2,1)} %a_hbm.1, s32[192,8]{1,0:T(8,128)S(1)} %copy.7.cols, bf16[192,64,192]{2,1,0:T(8,128)(2,1)} %p_hbm.1, s32[192,3]{1,0:T(8,128)S(1)} %copy.8.pattern, s32[192]{0:T(256)S(1)} %copy-done), custom_call_target="tpu_custom_call" | custom-call | tf_op jit(solution)/shard_map/pallas_call | solution.py:328
  32.1 0.0 copy-done.1
  32.1 22.3 %shard_map.65 = bf16[8,64,192]{2,1,0:T(8,128)(2,1)S(1)} custom-call(f32[256,256]{1,0:T(8,128)S(1)} %shard_map.64.total, s32[64]{0:T(128)S(1)} %copy-done.1), custom_call_target="tpu_custom_call" | custom-call | tf_op jit(solution)/shard_map/pallas_call | solution.py:351
  54.4 0.7 %copy.10 = bf16[8,64,192]{2,1,0:T(8,128)(2,1)} copy(bf16[8,64,192]{2,1,0:T(8,128)(2,1)S(1)} %shard_map.65) | data formatting | bytes 393216
Async XLA Ops:
  0.0 32.1 %copy-start.1 = (s32[64]{0:T(128)S(1)}, s32[64]{0:T(128)}, u32[]{:S(2)}) copy-start(s32[64]{0:T(128)} %owner_map.1) | copy-start | bytes 772
  1.6 0.7 %copy-start = (s32[192]{0:T(256)S(1)}, s32[192]{0:T(256)}, u32[]{:S(2)}) copy-start(s32[192]{0:T(256)} %aggregate.1) | copy-start | bytes 2308
where the time goes:
time: 55.4 us; the launch traced here: 55.1 us
  Pallas kernels  52 us (94%)
  local copies, waits for them, and re-layouts  3 us (5%)
    pallas_call x1, Pallas kernels, shards(): pl.pallas_call(kernel, out_shape=jax.ShapeDtypeStruct((4 * nodes, 4 * nod...  29.7 us
    pallas_call x1, Pallas kernels, shards(): pl.pallas_call(functools.partial(gather_kernel, wide, narrow), out_shape=...  22.3 us
    unnamed x7, local copies, waits for them, and re-layouts  3 us

commit v1 on v0

v1 whole, which is shorter than its diff:
```python
import jax
import jax.numpy as jnp
from jax import lax
from jax.experimental import pallas as pl
from jax.experimental.pallas import tpu as pltpu
from jax.sharding import PartitionSpec as P

HR = 32
LW = 2
OWNMAX = 8
GROUP = 16
SPR = 8
TEAM = 8
AXES = ("wide", "narrow")
MESH = pl.DeviceIdType.MESH
BF16 = jnp.bfloat16
F32 = jnp.float32


def kernel(a_hbm, cols, p_hbm, pattern, aggregate, owners, out,
           a_v, p_v, pooled, applied, sums, packed, rim, rim_side, edge_out, edge_in,
           piece_out, piece_in, spread, mail_out, mail_in, table_v, table,
           a_sem, p_sem, rim_send, rim_recv, edge_send, edge_recv,
           piece_send, piece_recv, spread_send, spread_recv, mail_send, mail_recv, table_sem):
    rows, nodes = a_hbm.shape[0], a_hbm.shape[1]
    me = lax.axis_index(AXES)
    narrow = lax.axis_size("narrow")
    count = lax.axis_size(AXES)
    teams = count // TEAM
    team, seat = me // TEAM, lax.rem(me, TEAM)
    groups = rows // GROUP

    def place_of(device):
        return (device // narrow, lax.rem(device, narrow))

    def mate(d):
        return team * TEAM + lax.rem(seat + d, TEAM)

    def peer(d):
        return lax.rem(team + d, teams) * TEAM + seat

    around = [place_of(lax.rem(me + 1, count)), place_of(lax.rem(me + count - 1, count))]
    barrier = pltpu.get_barrier_semaphore()
    for other in around:
        pl.semaphore_signal(barrier, inc=1, device_id=other, device_id_type=MESH)

    @pl.loop(1, TEAM)
    def _(d):
        pl.semaphore_signal(barrier, inc=1, device_id=place_of(mate(d)), device_id_type=MESH)

    @pl.loop(1, teams)
    def _(d):
        pl.semaphore_signal(barrier, inc=1, device_id=place_of(peer(d)), device_id_type=MESH)

    def p_copy(g):
        span = pl.ds(g * GROUP, GROUP)
        return pltpu.make_async_copy(p_hbm.at[span], p_v.at[span], p_sem.at[g])

    def a_copy(g):
        span = pl.ds(g * GROUP, GROUP)
        return pltpu.make_async_copy(a_hbm.at[span], a_v.at[span], a_sem.at[g])

    ends = (0, 1, groups - 2, groups - 1)
    middle = tuple(range(2, groups - 2))
    inner = tuple(range(3, groups - 3))
    for g in ends + middle:
        p_copy(g).start()
    for g in inner + (0, groups - 1, 1, 2, groups - 3, groups - 2):
        a_copy(g).start()

    total_agg = owners.shape[1]
    down = lax.broadcasted_iota(jnp.int32, (total_agg, total_agg), 0)
    over = lax.broadcasted_iota(jnp.int32, (total_agg, total_agg), 1)
    owner_row = owners[...]
    owner_col = jnp.sum(jnp.where(down == over, owner_row, 0), axis=1, keepdims=True)
    rank = jnp.sum(jnp.where((owner_col == owner_row) & (over < down), 1, 0), axis=1, keepdims=True)
    wanted = lax.broadcasted_iota(jnp.int32, (total_agg, 128), 1) + team * (TEAM * OWNMAX)
    number = lax.broadcasted_iota(jnp.int32, (total_agg, 128), 0) + 1
    hit = (owner_col * OWNMAX + rank) == wanted
    found = jnp.sum(jnp.where(hit, number, 0), axis=0, keepdims=True)
    table_v[...] = jnp.broadcast_to(found, table_v.shape)
    table_copy = pltpu.make_async_copy(table_v, table, table_sem)
    table_copy.start()

    left = lax.broadcasted_iota(jnp.int32, (nodes, 128), 1) < 64
    lane = lax.broadcasted_iota(jnp.int32, (1, 128), 1) < 64

    def place_group(g, at_end):
        for j in range(GROUP):
            i = g * GROUP + j
            second = jnp.where(aggregate[i] - me * LW == 1, 1.0, 0.0)
            has0 = pattern[0, i].astype(F32)
            has2 = pattern[2, i].astype(F32)
            x0 = p_v[i, :, :128]
            x2 = p_v[i, :, 128:]
            swapped = jnp.concatenate([x0[:, 64:], x0[:, :64]], axis=1)
            mixed = jnp.concatenate([x2, x0[:, 64:]], axis=1)
            one = jnp.where(lane, second, second * has0).astype(BF16)
            two = jnp.where(lane, (1.0 - second) * has2, 1.0 - second).astype(BF16)
            pooled[HR + i, :, :128] = swapped * one + mixed * two
            if at_end:
                three = jnp.where(lane, (1.0 - second) * has0, second * has2).astype(BF16)
                pooled[HR + i, :, 128:] = jnp.concatenate([x0[:, :64], x2], axis=1) * three
            else:
                pooled[HR + i, :, 128:] = jnp.zeros_like(x0)

    def rim_copies(side):
        end = pl.ds(rows + HR - SPR if side == 0 else HR, SPR)
        pairs = (
            (packed.at[side], rim.at[side]),
            (pooled.at[end, :, pl.ds(128, 128)], rim_side.at[side]),
        )
        return [
            pltpu.make_async_remote_copy(
                src_ref=source,
                dst_ref=landing,
                send_sem=rim_send.at[side, half],
                recv_sem=rim_recv.at[side, half],
                device_id=around[side],
                device_id_type=MESH,
            )
            for half, (source, landing) in enumerate(pairs)
        ]

    for g in ends:
        p_copy(g).wait()

    @pl.loop(0, 2)
    def _(end):
        place_group(end * (groups - 1), True)

    @pl.loop(0, HR // 2)
    def _(i):
        for side, first in ((0, rows - HR), (1, 0)):
            packed[side, i] = jnp.concatenate(
                [p_v[first + i + k, :, 64:128] for k in (0, HR // 2)], axis=1
            )

    pl.semaphore_wait(barrier, 2 + TEAM - 1 + teams - 1)
    copies = rim_copies(0) + rim_copies(1)
    for copy in copies:
        copy.start()

    @pl.loop(0, 2)
    def _(end):
        place_group(1 + end * (groups - 3), False)

    @pl.loop(2, groups - 2)
    def _(g):
        p_copy(g).wait()
        place_group(g, False)

    sums[...] = jnp.zeros_like(sums)
    base = HR - me * rows

    def apply_rows(first, buffer, width):
        for j in range(GROUP):
            i = first + j
            stack = jnp.concatenate(
                [pooled[jnp.maximum(cols[k, i] + base, 0), :, :width] for k in range(8)], axis=0
            )
            product = jnp.dot(a_v[i], stack, preferred_element_type=F32)
            applied[buffer, j * nodes : (j + 1) * nodes, :width] = product.astype(BF16)

    def add_up(first, buffer, high, width):
        left_rows = pooled[pl.ds(HR + first, GROUP), :, :high].reshape(GROUP * nodes, high)
        sums[:high, :width] += lax.dot_general(
            left_rows, applied[buffer, :, :width], (((0,), (0,)), ((), ())),
            preferred_element_type=F32,
        )

    def run_pair(first, later, high, width):
        apply_rows(first, 0, width)
        apply_rows(later, 1, width)
        add_up(first, 0, high, width)
        add_up(later, 1, high, width)

    @pl.loop(0, len(inner) // 2)
    def _(step):
        g = inner[0] + 2 * step
        a_copy(g).wait()
        a_copy(g + 1).wait()
        run_pair(g * GROUP, (g + 1) * GROUP, 128, 128)

    for copy in copies:
        copy.wait()

    @pl.loop(0, HR // 2)
    def _(i):
        zero = jnp.zeros((nodes, 128), BF16)
        for side, first in enumerate((0, rows + HR)):
            both = rim[side, i]
            swapped = jnp.concatenate([both[:, 64:], both[:, :64]], axis=1)
            keep = left if side == 0 else ~left
            early, late = (both, swapped) if side == 0 else (swapped, both)
            for k, own in ((0, early), (HR // 2, late)):
                pooled[first + i + k, :, :128] = zero
                pooled[first + i + k, :, 128:] = jnp.where(keep, own, zero)

    @pl.loop(0, SPR)
    def _(i):
        for side, first in enumerate((HR - SPR, rows + HR)):
            pooled[first + i, :, :128] = rim_side[side, i]

    a_copy(0).wait()
    a_copy(groups - 1).wait()
    run_pair(0, (groups - 1) * GROUP, 256, 256)

    edge_out[0, :, :64] = sums[192:, :64]
    edge_out[0, :, 64:] = sums[192:, 192:]
    edge_out[1, :, :64] = sums[128:192, 128:192]
    edge_out[1, :, 64:] = sums[128:192, 64:128]
    edges = [
        pltpu.make_async_remote_copy(
            src_ref=edge_out.at[side],
            dst_ref=edge_in.at[side],
            send_sem=edge_send.at[side],
            recv_sem=edge_recv.at[side],
            device_id=around[side],
            device_id_type=MESH,
        )
        for side in range(2)
    ]
    for edge in edges:
        edge.start()

    @pl.loop(0, 2)
    def _(side):
        g = 1 + side * (groups - 4)
        a_copy(g).wait()
        a_copy(g + 1).wait()
        run_pair(g * GROUP, (g + 1) * GROUP, 128, 256)

    for edge in edges:
        edge.wait()
    table_copy.wait()

    before, after = edge_in[0], edge_in[1]
    front0 = jnp.concatenate([sums[64:128, 128:192], sums[64:128, 64:128]], axis=1) + before
    front1 = jnp.concatenate([sums[:64, 64:128], sums[:64, :64] + after[:, :64]], axis=1)
    tails = jnp.concatenate([sums[64:128, :64], sums[:64, 192:] + after[:, 64:]], axis=1)
    lines = nodes // TEAM
    for t, part in enumerate((front0, front1, tails)):
        piece_out[:, t * lines : (t + 1) * lines, :] = part.reshape(TEAM, lines, 128)
    piece_in[seat] = piece_out[seat]

    def piece_copy(d):
        there = lax.rem(seat + d, TEAM)
        return pltpu.make_async_remote_copy(
            src_ref=piece_out.at[there],
            dst_ref=piece_in.at[seat],
            send_sem=piece_send.at[d],
            recv_sem=piece_recv.at[d],
            device_id=place_of(mate(d)),
            device_id_type=MESH,
        )

    @pl.loop(1, TEAM)
    def _(d):
        piece_copy(d).start()

    @pl.loop(1, TEAM)
    def _(d):
        piece_copy(d).wait()

    for pair in range(TEAM // 2):
        one, two = piece_in[2 * pair], piece_in[2 * pair + 1]
        spread[team, 3 * pair] = one[: 2 * lines].astype(BF16)
        spread[team, 3 * pair + 1] = two[: 2 * lines].astype(BF16)
        spread[team, 3 * pair + 2] = jnp.concatenate(
            [one[2 * lines :], two[2 * lines :]], axis=0
        ).astype(BF16)

    def spread_copy(d):
        return pltpu.make_async_remote_copy(
            src_ref=spread.at[team],
            dst_ref=spread.at[team],
            send_sem=spread_send.at[d],
            recv_sem=spread_recv.at[d],
            device_id=place_of(peer(d)),
            device_id_type=MESH,
        )

    @pl.loop(1, teams)
    def _(d):
        spread_copy(d).start()

    @pl.loop(1, teams)
    def _(d):
        spread_copy(d).wait()

    def fill(there, box):
        fronts, ends_of = [], []
        for s in range(OWNMAX):
            entry = table[0, there * OWNMAX + s]
            agg = jnp.maximum(entry - 1, 0)
            source = agg // LW
            which = lax.rem(agg, LW)
            from_team = source // TEAM
            member = lax.rem(source, TEAM)
            pair, half = member // 2, lax.rem(member, 2)
            front = spread[from_team, 3 * pair + half].astype(F32)
            front = jnp.where(which == 1, front[lines:], front[:lines])
            fronts.append(jnp.where(entry > 0, front, 0.0))
            tail = spread[from_team, 3 * pair + 2].astype(F32)
            tail = jnp.where(half == 1, tail[lines:], tail[:lines])
            swapped = jnp.concatenate([tail[:, 64:], tail[:, :64]], axis=1)
            tail = jnp.where(which == s % 2, tail, swapped)
            ends_of.append(jnp.where(entry > 0, tail, 0.0))
        for k in range(OWNMAX // 2):
            box[k] = jnp.concatenate(fronts[2 * k : 2 * k + 2], axis=0).astype(BF16)
        low = lax.broadcasted_iota(jnp.int32, (lines, 128), 1) < 64
        tails = [jnp.where(low, ends_of[2 * k], ends_of[2 * k + 1]) for k in range(OWNMAX // 2)]
        for k in range(OWNMAX // 4):
            box[OWNMAX // 2 + k] = jnp.concatenate(tails[2 * k : 2 * k + 2], axis=0).astype(BF16)

    def mail_copy(d):
        return pltpu.make_async_remote_copy(
            src_ref=mail_out.at[d],
            dst_ref=mail_in.at[seat],
            send_sem=mail_send.at[d],
            recv_sem=mail_recv.at[d],
            device_id=place_of(mate(d)),
            device_id_type=MESH,
        )

    @pl.loop(1, TEAM)
    def _(d):
        fill(lax.rem(seat + d, TEAM), mail_out.at[d])
        mail_copy(d).start()

    fill(seat, mail_in.at[seat])

    @pl.loop(1, TEAM)
    def _(d):
        mail_copy(d).wait()

    for m in range(TEAM // 2):
        span = pl.ds(2 * lines * m, 2 * lines)
        for k in range(OWNMAX // 2):
            one, two = (mail_in[2 * m + q, k].astype(F32) for q in range(2))
            for h in range(2):
                part = slice(h * lines, (h + 1) * lines)
                out[2 * k + h, span, :128] = jnp.concatenate([one[part], two[part]], axis=0).astype(BF16)
        for k in range(OWNMAX // 4):
            one, two = (mail_in[2 * m + q, OWNMAX // 2 + k].astype(F32) for q in range(2))
            for h in range(2):
                part = slice(h * lines, (h + 1) * lines)
                both = jnp.concatenate([one[part], two[part]], axis=0).astype(BF16)
                out[4 * k + 2 * h, span, 128:] = both[:, :64]
                out[4 * k + 2 * h + 1, span, 128:] = both[:, 64:]


def shards(a_blocks, a_columns, p_blocks, p_pattern, aggregate, owner_map):
    rows, nodes = a_blocks.shape[:2]
    teams = lax.axis_size(AXES) // TEAM
    vmem = pl.BlockSpec(memory_space=pltpu.VMEM)
    smem = pl.BlockSpec(memory_space=pltpu.SMEM)
    hbm = pl.BlockSpec(memory_space=pl.ANY)
    groups = rows // GROUP
    lines = nodes // TEAM
    half = OWNMAX // 2 + OWNMAX // 4
    dma = pltpu.SemaphoreType.DMA
    return pl.pallas_call(
        kernel,
        out_shape=jax.ShapeDtypeStruct((OWNMAX, nodes, 3 * nodes), BF16),
        in_specs=[hbm, smem, hbm, smem, smem, vmem],
        out_specs=vmem,
        scratch_shapes=[
            pltpu.VMEM(a_blocks.shape, BF16),
            pltpu.VMEM(p_blocks.shape, BF16),
            pltpu.VMEM((rows + 2 * HR, nodes, 4 * nodes), BF16),
            pltpu.VMEM((2, GROUP * nodes, 4 * nodes), BF16),
            pltpu.VMEM((4 * nodes, 4 * nodes), F32),
            pltpu.VMEM((2, HR // 2, nodes, 2 * nodes), BF16),
            pltpu.VMEM((2, HR // 2, nodes, 2 * nodes), BF16),
            pltpu.VMEM((2, SPR, nodes, 2 * nodes), BF16),
            pltpu.VMEM((2, nodes, 2 * nodes), F32),
            pltpu.VMEM((2, nodes, 2 * nodes), F32),
            pltpu.VMEM((TEAM, 3 * lines, 128), F32),
            pltpu.VMEM((TEAM, 3 * lines, 128), F32),
            pltpu.VMEM((teams, 3 * TEAM // 2, 2 * lines, 128), BF16),
            pltpu.VMEM((TEAM, half, 2 * lines, 128), BF16),
            pltpu.VMEM((TEAM, half, 2 * lines, 128), BF16),
            pltpu.VMEM((8, 128), jnp.int32),
            pltpu.SMEM((8, 128), jnp.int32),
            dma((groups,)),
            dma((groups,)),
            dma((2, 2)),
            dma((2, 2)),
            dma((2,)),
            dma((2,)),
            dma((TEAM,)),
            dma((TEAM,)),
            dma((teams,)),
            dma((teams,)),
            dma((TEAM,)),
            dma((TEAM,)),
            dma,
        ],
        compiler_params=pltpu.CompilerParams(
            collective_id=0, has_side_effects=True, vmem_limit_bytes=56 << 20
        ),
    )(a_blocks, a_columns.T, p_blocks, p_pattern.T, aggregate, owner_map[None])


def solution(mesh):
    placed = (
        P(AXES, None, None),
        P(AXES, None),
        P(AXES, None, None),
        P(AXES, None),
        P(AXES),
        P(),
    )
    return jax.shard_map(
        shards,
        mesh=mesh,
        in_specs=placed,
        out_specs=P(AXES, None, None),
        check_vma=False,
    )
```

time: 55.4 us -> 42.3 us (0.76)
  Pallas kernels: 52 us -> 40.4 us
  local copies, waits for them, and re-layouts: 3 us -> 1.67 us
    pallas_call x2 -> x1, Pallas kernels: 52 us -> 40.4 us  [shards(): pl.pallas_call(kernel, out_shape=jax.ShapeDtypeStruct((OWNMAX, nodes, 3 *...]
    unnamed x7 -> x1, local copies, waits for them, and re-layouts: 3 us -> 1.67 us
where the time goes in v1:
time: 42.3 us; the launch traced here: 42.1 us
  Pallas kernels  40.4 us (96%)
  local copies, waits for them, and re-layouts  1.67 us (4%)
    pallas_call x1, Pallas kernels, shards(): pl.pallas_call(kernel, out_shape=jax.ShapeDtypeStruct((OWNMAX, nodes, 3 *...  40.4 us
    unnamed x1, local copies, waits for them, and re-layouts  1.67 us

profile of v1, /device:TPU:0, one launch (start us, length us, event | category | flops | bytes accessed | tf_op | source)
XLA Modules:
  0.0 42.1 jit_solution(8843292767118142703)
XLA Ops:
  0.0 40.4 %shard_map.64 = bf16[8,64,192]{2,1,0:T(8,128)(2,1)} custom-call(bf16[192,64,512]{2,1,0:T(8,128)(2,1)} %a_hbm.1, s32[8,192]{1,0:T(8,128)} %bitcast.3, bf16[192,64,192]{2,1,0:T(8,128)(2,1)} %p_hbm.1, s32[3,192]{1,0:T(4,128)} %bitcast.4, s32[192]{0:T(256)} %aggregate.1, s32[1,64]{1,0:T(1,128)} %bitcast.5), custom_call_target="tpu_custom_call" | custom-call | tf_op jit(solution)/shard_map/pallas_call | solution.py:364
  40.4 1.7 %copy.8 = bf16[8,64,192]{2,1,0:T(8,128)(2,1)} copy(bf16[8,64,192]{2,1,0:T(8,128)(2,1)} %shard_map.64) | data formatting | bytes 393216

commit v2 on v1

v2 whole, which is shorter than its diff:
```python
import jax
import jax.numpy as jnp
from jax import lax
from jax.experimental import pallas as pl
from jax.experimental.pallas import tpu as pltpu
from jax.sharding import PartitionSpec as P

HR = 32
LW = 2
OWNMAX = 8
GROUP = 16
SPR = 8
TEAM = 8
AXES = ("wide", "narrow")
MESH = pl.DeviceIdType.MESH
BF16 = jnp.bfloat16
F32 = jnp.float32


def kernel(a_hbm, cols_hbm, p_hbm, pattern_hbm, aggregate_hbm, owners_hbm, out,
           cols, pattern, aggregate, owners, a_v, p_v, pooled, applied, sums, packed, packed_side,
           rim, rim_side, edge_out, edge_in, piece_out, spread, mail_out, mail_in, table_v, table,
           a_sem, p_sem, index_sem, rim_send, rim_recv, edge_send, edge_recv,
           piece_send, piece_recv, mail_send, mail_recv, vouch):
    rows, nodes = a_hbm.shape[0], a_hbm.shape[1]
    me = lax.axis_index(AXES)
    narrow = lax.axis_size("narrow")
    count = lax.axis_size(AXES)
    teams = count // TEAM
    rounds = teams.bit_length() - 1
    team, seat = me // TEAM, lax.rem(me, TEAM)
    groups = rows // GROUP
    has_before, has_after = me > 0, me < count - 1

    def place_of(device):
        return (device // narrow, lax.rem(device, narrow))

    def mate(d):
        return team * TEAM + lax.rem(seat + d, TEAM)

    def partner(r):
        step = 1 << r
        up = lax.rem(team // step, 2) == 0
        return place_of(jnp.where(up, team + step, team - step) * TEAM + seat)

    after = place_of(jnp.minimum(me + 1, count - 1))
    before = place_of(jnp.maximum(me - 1, 0))
    barrier = pltpu.get_barrier_semaphore()

    @pl.when(has_after)
    def _():
        pl.semaphore_signal(barrier, inc=1, device_id=after, device_id_type=MESH)

    @pl.when(has_before)
    def _():
        pl.semaphore_signal(barrier, inc=1, device_id=before, device_id_type=MESH)

    for r in range(rounds):
        pl.semaphore_signal(barrier, inc=1, device_id=partner(r), device_id_type=MESH)

    @pl.loop(1, TEAM)
    def _(d):
        pl.semaphore_signal(barrier, inc=1, device_id=place_of(mate(d)), device_id_type=MESH)

    def p_copy(g):
        span = pl.ds(g * GROUP, GROUP)
        return pltpu.make_async_copy(p_hbm.at[span], p_v.at[span], p_sem.at[g])

    def a_copy(g):
        span = pl.ds(g * GROUP, GROUP)
        return pltpu.make_async_copy(a_hbm.at[span], a_v.at[span], a_sem.at[g])

    index_copies = [
        pltpu.make_async_copy(source, landing, index_sem.at[k])
        for k, (source, landing) in enumerate(
            (
                (pattern_hbm, pattern),
                (aggregate_hbm, aggregate),
                (owners_hbm, owners),
                (cols_hbm, cols),
            )
        )
    ]
    for copy in index_copies:
        copy.start()
    ends = (0, 1, groups - 2, groups - 1)
    middle = tuple(range(2, groups - 2))
    inner = tuple(range(3, groups - 3))
    for g in ends + middle:
        p_copy(g).start()
    for g in inner + (2, groups - 3, 0, groups - 1, 1, groups - 2):
        a_copy(g).start()

    left = lax.broadcasted_iota(jnp.int32, (nodes, 128), 1) < 64
    lane = lax.broadcasted_iota(jnp.int32, (1, 128), 1) < 64

    def place_group(g, at_end):
        for j in range(GROUP):
            i = g * GROUP + j
            second = jnp.where(aggregate[0, i] - me * LW == 1, 1.0, 0.0)
            has0 = pattern[0, i].astype(F32)
            has2 = pattern[2, i].astype(F32)
            x0 = p_v[i, :, :128]
            x2 = p_v[i, :, 128:]
            swapped = jnp.concatenate([x0[:, 64:], x0[:, :64]], axis=1)
            mixed = jnp.concatenate([x2, x0[:, 64:]], axis=1)
            one = jnp.where(lane, second, second * has0).astype(BF16)
            two = jnp.where(lane, (1.0 - second) * has2, 1.0 - second).astype(BF16)
            pooled[HR + i, :, :128] = swapped * one + mixed * two
            if at_end:
                three = jnp.where(lane, (1.0 - second) * has0, second * has2).astype(BF16)
                pooled[HR + i, :, 128:] = jnp.concatenate([x0[:, :64], x2], axis=1) * three
            else:
                pooled[HR + i, :, 128:] = jnp.zeros_like(x0)

    for copy in index_copies:
        copy.wait()

    total_agg = owners.shape[1]
    down = lax.broadcasted_iota(jnp.int32, (total_agg, total_agg), 0)
    over = lax.broadcasted_iota(jnp.int32, (total_agg, total_agg), 1)
    owner_row = owners[...]
    owner_col = jnp.sum(jnp.where(down == over, owner_row, 0), axis=1, keepdims=True)
    rank = jnp.sum(jnp.where((owner_col == owner_row) & (over < down), 1, 0), axis=1, keepdims=True)
    wanted = lax.broadcasted_iota(jnp.int32, (total_agg, 128), 1) + team * (TEAM * OWNMAX)
    number = lax.broadcasted_iota(jnp.int32, (total_agg, 128), 0) + 1
    hit = (owner_col * OWNMAX + rank) == wanted
    found = jnp.sum(jnp.where(hit, number, 0), axis=0, keepdims=True)
    table_v[...] = jnp.broadcast_to(found, table_v.shape)
    table_copy = pltpu.make_async_copy(table_v, table, index_sem.at[4])
    table_copy.start()

    for g in ends:
        p_copy(g).wait()

    @pl.loop(0, 2)
    def _(end):
        place_group(end * (groups - 1), True)

    @pl.loop(0, HR // 2)
    def _(i):
        for side, first in ((0, rows - HR), (1, 0)):
            packed[side, i] = jnp.concatenate(
                [p_v[first + i + k, :, 64:128] for k in (0, HR // 2)], axis=1
            )

    @pl.loop(0, SPR // 2)
    def _(i):
        for side, first, at in ((0, HR + rows - SPR, 192), (1, HR, 128)):
            packed_side[side, i] = jnp.concatenate(
                [pooled[first + i + k, :, at : at + 64] for k in (0, SPR // 2)], axis=1
            )

    near = TEAM - 1 + rounds + jnp.where(has_after, 1, 0) + jnp.where(has_before, 1, 0)
    pl.semaphore_wait(barrier, near)

    def rim_copies(side):
        pairs = ((packed.at[side], rim.at[side]), (packed_side.at[side], rim_side.at[side]))
        return [
            pltpu.make_async_remote_copy(
                src_ref=source,
                dst_ref=landing,
                send_sem=rim_send.at[side, half],
                recv_sem=rim_recv.at[side, half],
                device_id=(after, before)[side],
                device_id_type=MESH,
            )
            for half, (source, landing) in enumerate(pairs)
        ]

    sends = (has_after, has_before)
    receives = (has_before, has_after)
    rims = [rim_copies(side) for side in range(2)]
    for side in range(2):
        @pl.when(sends[side])
        def _():
            for copy in rims[side]:
                copy.start()

    def vouch_for(r):
        pl.semaphore_signal(vouch.at[r], inc=1, device_id=partner(r), device_id_type=MESH)

    vouch_for(0)

    @pl.loop(0, 2)
    def _(end):
        place_group(1 + end * (groups - 3), False)

    @pl.loop(2, groups - 2)
    def _(g):
        p_copy(g).wait()
        place_group(g, False)

    @pl.loop(0, HR)
    def _(i):
        pooled[i] = jnp.zeros((nodes, 256), BF16)
        pooled[rows + HR + i] = jnp.zeros((nodes, 256), BF16)

    sums[...] = jnp.zeros_like(sums)
    base = HR - me * rows

    def apply_rows(first, total, buffer, width):
        for j in range(total):
            i = first + j
            stack = jnp.concatenate(
                [pooled[jnp.maximum(cols[k, i] + base, 0), :, :width] for k in range(8)], axis=0
            )
            product = jnp.dot(a_v[i], stack, preferred_element_type=F32)
            applied[buffer, j * nodes : (j + 1) * nodes, :width] = product.astype(BF16)

    def add_up(first, total, buffer, high, width):
        left_rows = pooled[pl.ds(HR + first, total), :, :high].reshape(total * nodes, high)
        sums[:high, :width] += lax.dot_general(
            left_rows, applied[buffer, : total * nodes, :width], (((0,), (0,)), ((), ())),
            preferred_element_type=F32,
        )

    def run_pair(first, later, total, high, width):
        apply_rows(first, total, 0, width)
        apply_rows(later, total, 1, width)
        add_up(first, total, 0, high, width)
        add_up(later, total, 1, high, width)

    @pl.loop(0, len(inner) // 2)
    def _(step):
        g = inner[0] + 2 * step
        a_copy(g).wait()
        a_copy(g + 1).wait()
        run_pair(g * GROUP, (g + 1) * GROUP, GROUP, 128, 128)

    pl.semaphore_wait(vouch.at[0], 1)
    for r in range(1, rounds):
        vouch_for(r)
        if r < rounds - 1:
            pl.semaphore_wait(vouch.at[r], 1)

    a_copy(2).wait()
    a_copy(groups - 3).wait()
    run_pair(2 * GROUP, (groups - 3) * GROUP, GROUP, 128, 256)
    for g in ends:
        a_copy(g).wait()

    zero = jnp.zeros((nodes, 128), BF16)
    for side, first in enumerate((0, rows + HR)):
        @pl.when(receives[side])
        def _():
            for copy in rims[side]:
                copy.wait_recv()
            keep = left if side == 0 else ~left

            @pl.loop(0, HR // 2)
            def _(i):
                both = rim[side, i]
                swapped = jnp.concatenate([both[:, 64:], both[:, :64]], axis=1)
                early, late = (both, swapped) if side == 0 else (swapped, both)
                for k, own in ((0, early), (HR // 2, late)):
                    pooled[first + i + k, :, 128:] = jnp.where(keep, own, zero)

            start = HR - SPR if side == 0 else rows + HR

            @pl.loop(0, SPR // 2)
            def _(i):
                both = rim_side[side, i]
                swapped = jnp.concatenate([both[:, 64:], both[:, :64]], axis=1)
                early, late = (swapped, both) if side == 0 else (both, swapped)
                for k, own in ((0, early), (SPR // 2, late)):
                    pooled[start + i + k, :, :128] = jnp.where(keep, zero, own)

    run_pair(0, rows - SPR, SPR, 256, 256)

    edge_out[0, :, :64] = sums[192:, :64]
    edge_out[0, :, 64:] = sums[192:, 192:]
    edge_out[1, :, :64] = sums[128:192, 128:192]
    edge_out[1, :, 64:] = sums[128:192, 64:128]
    edges = [
        pltpu.make_async_remote_copy(
            src_ref=edge_out.at[side],
            dst_ref=edge_in.at[side],
            send_sem=edge_send.at[side],
            recv_sem=edge_recv.at[side],
            device_id=(after, before)[side],
            device_id_type=MESH,
        )
        for side in range(2)
    ]
    for side in range(2):
        @pl.when(sends[side])
        def _():
            edges[side].start()

    @pl.loop(0, 2)
    def _(side):
        first = SPR + side * (rows - HR - SPR)
        apply_rows(first, HR - SPR, 0, 256)
        add_up(first, HR - SPR, 0, 128, 256)

    table_copy.wait()
    if rounds:
        pl.semaphore_wait(vouch.at[rounds - 1], 1)
    for side in range(2):
        @pl.when(receives[side])
        def _():
            edges[side].wait_recv()

        @pl.when(~receives[side])
        def _():
            edge_in[side] = jnp.zeros((nodes, 128), F32)

    early, late = edge_in[0], edge_in[1]
    front0 = jnp.concatenate([sums[64:128, 128:192], sums[64:128, 64:128]], axis=1) + early
    front1 = jnp.concatenate([sums[:64, 64:128], sums[:64, :64] + late[:, :64]], axis=1)
    tails = jnp.concatenate([sums[64:128, :64], sums[:64, 192:] + late[:, 64:]], axis=1)
    lines = nodes // TEAM
    for s in range(TEAM):
        part = slice(s * lines, (s + 1) * lines)
        piece_out[s, : 2 * lines] = jnp.concatenate([front0[part], front1[part]], axis=0).astype(BF16)
        piece_out[s, 2 * lines :] = tails[part].astype(BF16)

    def piece_copy(d):
        there = lax.rem(me + d, count)
        return pltpu.make_async_remote_copy(
            src_ref=piece_out.at[lax.rem(there, TEAM)],
            dst_ref=spread.at[me],
            send_sem=piece_send.at[d],
            recv_sem=piece_recv.at[d],
            device_id=place_of(there),
            device_id_type=MESH,
        )

    @pl.loop(1, count)
    def _(d):
        piece_copy(d).start()

    spread[me] = piece_out[seat]

    @pl.loop(1, count)
    def _(d):
        piece_copy(d).wait_recv()

    low = lax.broadcasted_iota(jnp.int32, (lines, 128), 1) < 64

    def fill(there, box):
        fronts, ends_of = [], []
        for s in range(OWNMAX):
            entry = table[0, there * OWNMAX + s]
            agg = jnp.maximum(entry - 1, 0)
            which = lax.rem(agg, LW)
            piece = spread[agg // LW].astype(F32)
            front = jnp.where(which == 1, piece[lines : 2 * lines], piece[:lines])
            fronts.append(jnp.where(entry > 0, front, 0.0))
            tail = piece[2 * lines :]
            swapped = jnp.concatenate([tail[:, 64:], tail[:, :64]], axis=1)
            tail = jnp.where(which == s % 2, tail, swapped)
            ends_of.append(jnp.where(entry > 0, tail, 0.0))
        for k in range(OWNMAX // 2):
            box[k] = jnp.concatenate(fronts[2 * k : 2 * k + 2], axis=0).astype(BF16)
        tails = [jnp.where(low, ends_of[2 * k], ends_of[2 * k + 1]) for k in range(OWNMAX // 2)]
        for k in range(OWNMAX // 4):
            box[OWNMAX // 2 + k] = jnp.concatenate(tails[2 * k : 2 * k + 2], axis=0).astype(BF16)

    def mail_copy(d):
        return pltpu.make_async_remote_copy(
            src_ref=mail_out.at[d],
            dst_ref=mail_in.at[seat],
            send_sem=mail_send.at[d],
            recv_sem=mail_recv.at[d],
            device_id=place_of(mate(d)),
            device_id_type=MESH,
        )

    @pl.loop(1, TEAM)
    def _(d):
        fill(lax.rem(seat + d, TEAM), mail_out.at[d])
        mail_copy(d).start()

    fill(seat, mail_in.at[seat])

    @pl.loop(1, TEAM)
    def _(d):
        mail_copy(d).wait_recv()

    for m in range(TEAM // 2):
        span = pl.ds(2 * lines * m, 2 * lines)
        for k in range(OWNMAX // 2):
            one, two = (mail_in[2 * m + q, k].astype(F32) for q in range(2))
            for h in range(2):
                part = slice(h * lines, (h + 1) * lines)
                out[2 * k + h, span, :128] = jnp.concatenate([one[part], two[part]], axis=0).astype(BF16)
        for k in range(OWNMAX // 4):
            one, two = (mail_in[2 * m + q, OWNMAX // 2 + k].astype(F32) for q in range(2))
            for h in range(2):
                part = slice(h * lines, (h + 1) * lines)
                both = jnp.concatenate([one[part], two[part]], axis=0).astype(BF16)
                out[4 * k + 2 * h, span, 128:] = both[:, :64]
                out[4 * k + 2 * h + 1, span, 128:] = both[:, 64:]

    for side in range(2):
        @pl.when(sends[side])
        def _():
            for copy in rims[side] + [edges[side]]:
                copy.wait_send()

    @pl.loop(1, count)
    def _(d):
        piece_copy(d).wait_send()

    @pl.loop(1, TEAM)
    def _(d):
        mail_copy(d).wait_send()


def shards(a_blocks, a_columns, p_blocks, p_pattern, aggregate, owner_map):
    rows, nodes = a_blocks.shape[:2]
    count = lax.axis_size(AXES)
    vmem = pl.BlockSpec(memory_space=pltpu.VMEM)
    hbm = pl.BlockSpec(memory_space=pl.ANY)
    groups = rows // GROUP
    lines = nodes // TEAM
    half = OWNMAX // 2 + OWNMAX // 4
    dma = pltpu.SemaphoreType.DMA
    pool = (rows + 2 * HR, nodes, 4 * nodes)
    total_agg = owner_map.shape[0]
    return pl.pallas_call(
        kernel,
        out_shape=jax.ShapeDtypeStruct((OWNMAX, nodes, 3 * nodes), BF16),
        in_specs=[hbm] * 6,
        out_specs=vmem,
        scratch_shapes=[
            pltpu.SMEM((a_columns.shape[1], rows), jnp.int32),
            pltpu.SMEM((3, rows), jnp.int32),
            pltpu.SMEM((1, rows), jnp.int32),
            pltpu.VMEM((1, total_agg), jnp.int32),
            pltpu.VMEM(a_blocks.shape, BF16),
            pltpu.VMEM(p_blocks.shape, BF16),
            pltpu.VMEM(pool, BF16),
            pltpu.VMEM((2, (HR - SPR) * nodes, 4 * nodes), BF16),
            pltpu.VMEM((4 * nodes, 4 * nodes), F32),
            pltpu.VMEM((2, HR // 2, nodes, 2 * nodes), BF16),
            pltpu.VMEM((2, SPR // 2, nodes, 2 * nodes), BF16),
            pltpu.VMEM((2, HR // 2, nodes, 2 * nodes), BF16),
            pltpu.VMEM((2, SPR // 2, nodes, 2 * nodes), BF16),
            pltpu.VMEM((2, nodes, 2 * nodes), F32),
            pltpu.VMEM((2, nodes, 2 * nodes), F32),
            pltpu.VMEM((TEAM, 3 * lines, 128), BF16),
            pltpu.VMEM((count, 3 * lines, 128), BF16),
            pltpu.VMEM((TEAM, half, 2 * lines, 128), BF16),
            pltpu.VMEM((TEAM, half, 2 * lines, 128), BF16),
            pltpu.VMEM((8, 128), jnp.int32),
            pltpu.SMEM((8, 128), jnp.int32),
            dma((groups,)),
            dma((groups,)),
            dma((5,)),
            dma((2, 2)),
            dma((2, 2)),
            dma((2,)),
            dma((2,)),
            dma((count,)),
            dma((count,)),
            dma((TEAM,)),
            dma((TEAM,)),
            pltpu.SemaphoreType.REGULAR((max(count // TEAM - 1, 1).bit_length(),)),
        ],
        compiler_params=pltpu.CompilerParams(
            collective_id=0, has_side_effects=True, vmem_limit_bytes=56 << 20
        ),
    )(a_blocks, a_columns.T, p_blocks, p_pattern.T, aggregate[None], owner_map[None])


def solution(mesh):
    placed = (
        P(AXES, None, None),
        P(AXES, None),
        P(AXES, None, None),
        P(AXES, None),
        P(AXES),
        P(),
    )
    return jax.shard_map(
        shards,
        mesh=mesh,
        in_specs=placed,
        out_specs=P(AXES, None, None),
        check_vma=False,
    )
```

time: 42.3 us -> 40.3 us (0.953)
  Pallas kernels: 40.4 us -> 38.4 us
    pallas_call x1, Pallas kernels: 40.4 us -> 38.4 us  [shards(): pl.pallas_call(kernel, out_shape=jax.ShapeDtypeStruct((OWNMAX, nodes, 3 *...]
where the time goes in v2:
time: 40.3 us; the launch traced here: 40.1 us
  Pallas kernels  38.4 us (95%)
  local copies, waits for them, and re-layouts  1.67 us (4%)
    pallas_call x1, Pallas kernels, shards(): pl.pallas_call(kernel, out_shape=jax.ShapeDtypeStruct((OWNMAX, nodes, 3 *...  38.4 us
    unnamed x1, local copies, waits for them, and re-layouts  1.67 us

profile of v2, /device:TPU:0, one launch (start us, length us, event | category | flops | bytes accessed | tf_op | source)
XLA Modules:
  0.0 40.1 jit_solution(8773303948554842018)
XLA Ops:
  0.0 38.4 %shard_map.64 = bf16[8,64,192]{2,1,0:T(8,128)(2,1)} custom-call(bf16[192,64,512]{2,1,0:T(8,128)(2,1)} %a_hbm.1, s32[8,192]{1,0:T(8,128)} %bitcast.4, bf16[192,64,192]{2,1,0:T(8,128)(2,1)} %p_hbm.1, s32[3,192]{1,0:T(4,128)} %bitcast.5, s32[1,192]{1,0:T(1,128)} %bitcast.6, s32[1,64]{1,0:T(1,128)} %bitcast.7), custom_call_target="tpu_custom_call" | custom-call | tf_op jit(solution)/shard_map/pallas_call | solution.py:423
  38.4 1.7 %copy.8 = bf16[8,64,192]{2,1,0:T(8,128)(2,1)} copy(bf16[8,64,192]{2,1,0:T(8,128)(2,1)} %shard_map.64) | data formatting | bytes 393216

commit v3 on v2

--- a/solution.py
+++ b/solution.py
@@ -86,10 +86,8 @@
     ends = (0, 1, groups - 2, groups - 1)
     middle = tuple(range(2, groups - 2))
     inner = tuple(range(3, groups - 3))
-    for g in ends + middle:
+    for g in ends:
         p_copy(g).start()
-    for g in inner + (2, groups - 3, 0, groups - 1, 1, groups - 2):
-        a_copy(g).start()
 
     left = lax.broadcasted_iota(jnp.int32, (nodes, 128), 1) < 64
     lane = lax.broadcasted_iota(jnp.int32, (1, 128), 1) < 64
@@ -132,6 +130,10 @@
 
     for g in ends:
         p_copy(g).wait()
+    for g in middle:
+        p_copy(g).start()
+    for g in inner + (2, groups - 3, 0, groups - 1, 1, groups - 2):
+        a_copy(g).start()
 
     @pl.loop(0, 2)
     def _(end):
@@ -248,7 +250,7 @@
                 copy.wait_recv()
             keep = left if side == 0 else ~left
 
-            @pl.loop(0, HR // 2)
+            @pl.loop(0, HR // 2, unroll=4)
             def _(i):
                 both = rim[side, i]
                 swapped = jnp.concatenate([both[:, 64:], both[:, :64]], axis=1)
@@ -258,7 +260,7 @@
 
             start = HR - SPR if side == 0 else rows + HR
 
-            @pl.loop(0, SPR // 2)
+            @pl.loop(0, SPR // 2, unroll=2)
             def _(i):
                 both = rim_side[side, i]
                 swapped = jnp.concatenate([both[:, 64:], both[:, :64]], axis=1)

time: 40.3 us -> 35.5 us (0.88)
  Pallas kernels: 38.4 us -> 33.6 us
    pallas_call x1, Pallas kernels: 38.4 us -> 33.6 us  [shards(): pl.pallas_call(kernel, out_shape=jax.ShapeDtypeStruct((OWNMAX, nodes, 3 *...]
where the time goes in v3:
time: 35.5 us; the launch traced here: 35.3 us
  Pallas kernels  33.6 us (95%)
  local copies, waits for them, and re-layouts  1.67 us (5%)
    pallas_call x1, Pallas kernels, shards(): pl.pallas_call(kernel, out_shape=jax.ShapeDtypeStruct((OWNMAX, nodes, 3 *...  33.6 us
    unnamed x1, local copies, waits for them, and re-layouts  1.67 us

profile of v3, /device:TPU:0, one launch (start us, length us, event | category | flops | bytes accessed | tf_op | source)
XLA Modules:
  0.0 35.3 jit_solution(15415859398450627685)
XLA Ops:
  0.0 33.6 %shard_map.64 = bf16[8,64,192]{2,1,0:T(8,128)(2,1)} custom-call(bf16[192,64,512]{2,1,0:T(8,128)(2,1)} %a_hbm.1, s32[8,192]{1,0:T(8,128)} %bitcast.4, bf16[192,64,192]{2,1,0:T(8,128)(2,1)} %p_hbm.1, s32[3,192]{1,0:T(4,128)} %bitcast.5, s32[1,192]{1,0:T(1,128)} %bitcast.6, s32[1,64]{1,0:T(1,128)} %bitcast.7), custom_call_target="tpu_custom_call" | custom-call | tf_op jit(solution)/shard_map/pallas_call | solution.py:425
  33.6 1.7 %copy.8 = bf16[8,64,192]{2,1,0:T(8,128)(2,1)} copy(bf16[8,64,192]{2,1,0:T(8,128)(2,1)} %shard_map.64) | data formatting | bytes 393216

commit v4 on v3

--- a/solution.py
+++ b/solution.py
@@ -18,8 +18,8 @@
 
 
 def kernel(a_hbm, cols_hbm, p_hbm, pattern_hbm, aggregate_hbm, owners_hbm, out,
-           cols, pattern, aggregate, owners, a_v, p_v, pooled, applied, sums, packed, packed_side,
-           rim, rim_side, edge_out, edge_in, piece_out, spread, mail_out, mail_in, table_v, table,
+           cols, pattern, aggregate, owners, a_v, p_v, pooled, applied, sums, packed, rim,
+           edge_out, edge_in, piece_out, spread, mail_out, mail_in, table_v, table,
            a_sem, p_sem, index_sem, rim_send, rim_recv, edge_send, edge_recv,
            piece_send, piece_recv, mail_send, mail_recv, vouch):
     rows, nodes = a_hbm.shape[0], a_hbm.shape[1]
@@ -62,13 +62,24 @@
     def _(d):
         pl.semaphore_signal(barrier, inc=1, device_id=place_of(mate(d)), device_id_type=MESH)
 
-    def p_copy(g):
-        span = pl.ds(g * GROUP, GROUP)
-        return pltpu.make_async_copy(p_hbm.at[span], p_v.at[span], p_sem.at[g])
-
-    def a_copy(g):
-        span = pl.ds(g * GROUP, GROUP)
-        return pltpu.make_async_copy(a_hbm.at[span], a_v.at[span], a_sem.at[g])
+    step = 2 * GROUP
+
+    def p_copy(k):
+        first = (0, rows - step, step, rows // 2)[k]
+        span = pl.ds(first, step if k < 2 else rows // 2 - step)
+        return pltpu.make_async_copy(p_hbm.at[span], p_v.at[span], p_sem.at[k])
+
+    wing = rows // 4
+    inner = (rows - 2 * wing) // step
+
+    def a_copy(first, total, k):
+        span = pl.ds(first, total)
+        return pltpu.make_async_copy(a_hbm.at[span], a_v.at[span], a_sem.at[k])
+
+    def a_inner(k):
+        return a_copy(wing + k * step, step, k)
+
+    a_wings = [a_copy(first, wing, inner + k) for k, first in enumerate((0, rows - wing))]
 
     index_copies = [
         pltpu.make_async_copy(source, landing, index_sem.at[k])
@@ -83,11 +94,8 @@
     ]
     for copy in index_copies:
         copy.start()
-    ends = (0, 1, groups - 2, groups - 1)
-    middle = tuple(range(2, groups - 2))
-    inner = tuple(range(3, groups - 3))
-    for g in ends:
-        p_copy(g).start()
+    for k in range(2):
+        p_copy(k).start()
 
     left = lax.broadcasted_iota(jnp.int32, (nodes, 128), 1) < 64
     lane = lax.broadcasted_iota(jnp.int32, (1, 128), 1) < 64
@@ -128,12 +136,14 @@
     table_copy = pltpu.make_async_copy(table_v, table, index_sem.at[4])
     table_copy.start()
 
-    for g in ends:
-        p_copy(g).wait()
-    for g in middle:
-        p_copy(g).start()
-    for g in inner + (2, groups - 3, 0, groups - 1, 1, groups - 2):
-        a_copy(g).start()
+    for k in range(2):
+        p_copy(k).wait()
+    for k in range(2, 4):
+        p_copy(k).start()
+    for k in range(inner):
+        a_inner(k).start()
+    for copy in a_wings:
+        copy.start()
 
     @pl.loop(0, 2)
     def _(end):
@@ -149,49 +159,13 @@
     @pl.loop(0, SPR // 2)
     def _(i):
         for side, first, at in ((0, HR + rows - SPR, 192), (1, HR, 128)):
-            packed_side[side, i] = jnp.concatenate(
+            packed[side, HR // 2 + i] = jnp.concatenate(
                 [pooled[first + i + k, :, at : at + 64] for k in (0, SPR // 2)], axis=1
             )
-
-    near = TEAM - 1 + rounds + jnp.where(has_after, 1, 0) + jnp.where(has_before, 1, 0)
-    pl.semaphore_wait(barrier, near)
-
-    def rim_copies(side):
-        pairs = ((packed.at[side], rim.at[side]), (packed_side.at[side], rim_side.at[side]))
-        return [
-            pltpu.make_async_remote_copy(
-                src_ref=source,
-                dst_ref=landing,
-                send_sem=rim_send.at[side, half],
-                recv_sem=rim_recv.at[side, half],
-                device_id=(after, before)[side],
-                device_id_type=MESH,
-            )
-            for half, (source, landing) in enumerate(pairs)
-        ]
-
-    sends = (has_after, has_before)
-    receives = (has_before, has_after)
-    rims = [rim_copies(side) for side in range(2)]
-    for side in range(2):
-        @pl.when(sends[side])
-        def _():
-            for copy in rims[side]:
-                copy.start()
-
-    def vouch_for(r):
-        pl.semaphore_signal(vouch.at[r], inc=1, device_id=partner(r), device_id_type=MESH)
-
-    vouch_for(0)
 
     @pl.loop(0, 2)
     def _(end):
         place_group(1 + end * (groups - 3), False)
-
-    @pl.loop(2, groups - 2)
-    def _(g):
-        p_copy(g).wait()
-        place_group(g, False)
 
     @pl.loop(0, HR)
     def _(i):
@@ -199,6 +173,41 @@
         pooled[rows + HR + i] = jnp.zeros((nodes, 256), BF16)
 
     sums[...] = jnp.zeros_like(sums)
+    near = TEAM - 1 + rounds + jnp.where(has_after, 1, 0) + jnp.where(has_before, 1, 0)
+    pl.semaphore_wait(barrier, near)
+
+    def both_ways(outbox, inbox, send_sem, recv_sem):
+        return [
+            pltpu.make_async_remote_copy(
+                src_ref=outbox.at[side],
+                dst_ref=inbox.at[side],
+                send_sem=send_sem.at[side],
+                recv_sem=recv_sem.at[side],
+                device_id=(after, before)[side],
+                device_id_type=MESH,
+            )
+            for side in range(2)
+        ]
+
+    sends = (has_after, has_before)
+    receives = (has_before, has_after)
+    rims = both_ways(packed, rim, rim_send, rim_recv)
+    for side in range(2):
+        @pl.when(sends[side])
+        def _():
+            rims[side].start()
+
+    def vouch_for(r):
+        pl.semaphore_signal(vouch.at[r], inc=1, device_id=partner(r), device_id_type=MESH)
+
+    vouch_for(0)
+    for k in range(2, 4):
+        p_copy(k).wait()
+
+    @pl.loop(2, groups - 2)
+    def _(g):
+        place_group(g, False)
+
     base = HR - me * rows
 
     def apply_rows(first, total, buffer, width):
@@ -223,31 +232,26 @@
         add_up(first, total, 0, high, width)
         add_up(later, total, 1, high, width)
 
-    @pl.loop(0, len(inner) // 2)
-    def _(step):
-        g = inner[0] + 2 * step
-        a_copy(g).wait()
-        a_copy(g + 1).wait()
-        run_pair(g * GROUP, (g + 1) * GROUP, GROUP, 128, 128)
+    @pl.loop(0, inner)
+    def _(k):
+        a_inner(k).wait()
+        first = wing + k * step
+        run_pair(first, first + GROUP, GROUP, 128, 128)
 
     pl.semaphore_wait(vouch.at[0], 1)
     for r in range(1, rounds):
         vouch_for(r)
         if r < rounds - 1:
             pl.semaphore_wait(vouch.at[r], 1)
-
-    a_copy(2).wait()
-    a_copy(groups - 3).wait()
-    run_pair(2 * GROUP, (groups - 3) * GROUP, GROUP, 128, 256)
-    for g in ends:
-        a_copy(g).wait()
+    for copy in a_wings:
+        copy.wait()
+    run_pair(HR, rows - HR - GROUP, GROUP, 128, 256)
 
     zero = jnp.zeros((nodes, 128), BF16)
     for side, first in enumerate((0, rows + HR)):
         @pl.when(receives[side])
         def _():
-            for copy in rims[side]:
-                copy.wait_recv()
+            rims[side].wait_recv()
             keep = left if side == 0 else ~left
 
             @pl.loop(0, HR // 2, unroll=4)
@@ -262,7 +266,7 @@
 
             @pl.loop(0, SPR // 2, unroll=2)
             def _(i):
-                both = rim_side[side, i]
+                both = rim[side, HR // 2 + i]
                 swapped = jnp.concatenate([both[:, 64:], both[:, :64]], axis=1)
                 early, late = (swapped, both) if side == 0 else (both, swapped)
                 for k, own in ((0, early), (SPR // 2, late)):
@@ -274,17 +278,7 @@
     edge_out[0, :, 64:] = sums[192:, 192:]
     edge_out[1, :, :64] = sums[128:192, 128:192]
     edge_out[1, :, 64:] = sums[128:192, 64:128]
-    edges = [
-        pltpu.make_async_remote_copy(
-            src_ref=edge_out.at[side],
-            dst_ref=edge_in.at[side],
-            send_sem=edge_send.at[side],
-            recv_sem=edge_recv.at[side],
-            device_id=(after, before)[side],
-            device_id_type=MESH,
-        )
-        for side in range(2)
-    ]
+    edges = both_ways(edge_out, edge_in, edge_send, edge_recv)
     for side in range(2):
         @pl.when(sends[side])
         def _():
@@ -323,8 +317,8 @@
         return pltpu.make_async_remote_copy(
             src_ref=piece_out.at[lax.rem(there, TEAM)],
             dst_ref=spread.at[me],
-            send_sem=piece_send.at[d],
-            recv_sem=piece_recv.at[d],
+            send_sem=piece_send,
+            recv_sem=piece_recv,
             device_id=place_of(there),
             device_id_type=MESH,
         )
@@ -335,9 +329,12 @@
 
     spread[me] = piece_out[seat]
 
-    @pl.loop(1, count)
-    def _(d):
-        piece_copy(d).wait_recv()
+    others = spread.at[pl.ds(0, count - 1)]
+    all_pieces = pltpu.make_async_remote_copy(
+        src_ref=others, dst_ref=others, send_sem=piece_send, recv_sem=piece_recv,
+        device_id=after, device_id_type=MESH,
+    )
+    all_pieces.wait_recv()
 
     low = lax.broadcasted_iota(jnp.int32, (lines, 128), 1) < 64
 
@@ -364,8 +361,8 @@
         return pltpu.make_async_remote_copy(
             src_ref=mail_out.at[d],
             dst_ref=mail_in.at[seat],
-            send_sem=mail_send.at[d],
-            recv_sem=mail_recv.at[d],
+            send_sem=mail_send,
+            recv_sem=mail_recv,
             device_id=place_of(mate(d)),
             device_id_type=MESH,
         )
@@ -377,9 +374,12 @@
 
     fill(seat, mail_in.at[seat])
 
-    @pl.loop(1, TEAM)
-    def _(d):
-        mail_copy(d).wait_recv()
+    boxes = mail_in.at[pl.ds(0, TEAM - 1)]
+    all_mail = pltpu.make_async_remote_copy(
+        src_ref=boxes, dst_ref=boxes, send_sem=mail_send, recv_sem=mail_recv,
+        device_id=after, device_id_type=MESH,
+    )
+    all_mail.wait_recv()
 
     for m in range(TEAM // 2):
         span = pl.ds(2 * lines * m, 2 * lines)
@@ -399,16 +399,12 @@
     for side in range(2):
         @pl.when(sends[side])
         def _():
-            for copy in rims[side] + [edges[side]]:
-                copy.wait_send()
-
-    @pl.loop(1, count)
-    def _(d):
-        piece_copy(d).wait_send()
-
-    @pl.loop(1, TEAM)
-    def _(d):
-        mail_copy(d).wait_send()
+            rims[side].wait_send()
+            edges[side].wait_send()
+
+    all_pieces.wait_send()
+
+    all_mail.wait_send()
 
 
 def shards(a_blocks, a_columns, p_blocks, p_pattern, aggregate, owner_map):
@@ -416,7 +412,6 @@
     count = lax.axis_size(AXES)
     vmem = pl.BlockSpec(memory_space=pltpu.VMEM)
     hbm = pl.BlockSpec(memory_space=pl.ANY)
-    groups = rows // GROUP
     lines = nodes // TEAM
     half = OWNMAX // 2 + OWNMAX // 4
     dma = pltpu.SemaphoreType.DMA
@@ -437,10 +432,8 @@
             pltpu.VMEM(pool, BF16),
             pltpu.VMEM((2, (HR - SPR) * nodes, 4 * nodes), BF16),
             pltpu.VMEM((4 * nodes, 4 * nodes), F32),
-            pltpu.VMEM((2, HR // 2, nodes, 2 * nodes), BF16),
-            pltpu.VMEM((2, SPR // 2, nodes, 2 * nodes), BF16),
-            pltpu.VMEM((2, HR // 2, nodes, 2 * nodes), BF16),
-            pltpu.VMEM((2, SPR // 2, nodes, 2 * nodes), BF16),
+            pltpu.VMEM((2, (HR + SPR) // 2, nodes, 2 * nodes), BF16),
+            pltpu.VMEM((2, (HR + SPR) // 2, nodes, 2 * nodes), BF16),
             pltpu.VMEM((2, nodes, 2 * nodes), F32),
             pltpu.VMEM((2, nodes, 2 * nodes), F32),
             pltpu.VMEM((TEAM, 3 * lines, 128), BF16),
@@ -449,17 +442,17 @@
             pltpu.VMEM((TEAM, half, 2 * lines, 128), BF16),
             pltpu.VMEM((8, 128), jnp.int32),
             pltpu.SMEM((8, 128), jnp.int32),
-            dma((groups,)),
-            dma((groups,)),
+            dma((rows // 4 // GROUP + 2,)),
+            dma((4,)),
             dma((5,)),
-            dma((2, 2)),
-            dma((2, 2)),
             dma((2,)),
             dma((2,)),
-            dma((count,)),
-            dma((count,)),
-            dma((TEAM,)),
-            dma((TEAM,)),
+            dma((2,)),
+            dma((2,)),
+            dma,
+            dma,
+            dma,
+            dma,
             pltpu.SemaphoreType.REGULAR((max(count // TEAM - 1, 1).bit_length(),)),
         ],
         compiler_params=pltpu.CompilerParams(

time: 35.5 us -> 34.6 us (0.975)
  Pallas kernels: 33.6 us -> 32.8 us
    pallas_call x1, Pallas kernels: 33.6 us -> 32.8 us  [shards(): pl.pallas_call(kernel, out_shape=jax.ShapeDtypeStruct((OWNMAX, nodes, 3 *...]
where the time goes in v4:
time: 34.6 us; the launch traced here: 34.4 us
  Pallas kernels  32.8 us (95%)
  local copies, waits for them, and re-layouts  1.67 us (5%)
    pallas_call x1, Pallas kernels, shards(): pl.pallas_call(kernel, out_shape=jax.ShapeDtypeStruct((OWNMAX, nodes, 3 *...  32.8 us
    unnamed x1, local copies, waits for them, and re-layouts  1.67 us

profile of v4, /device:TPU:0, one launch (start us, length us, event | category | flops | bytes accessed | tf_op | source)
XLA Modules:
  0.0 34.4 jit_solution(16409196092337234019)
XLA Ops:
  0.0 32.8 %shard_map.64 = bf16[8,64,192]{2,1,0:T(8,128)(2,1)} custom-call(bf16[192,64,512]{2,1,0:T(8,128)(2,1)} %a_hbm.1, s32[8,192]{1,0:T(8,128)} %bitcast.4, bf16[192,64,192]{2,1,0:T(8,128)(2,1)} %p_hbm.1, s32[3,192]{1,0:T(4,128)} %bitcast.5, s32[1,192]{1,0:T(1,128)} %bitcast.6, s32[1,64]{1,0:T(1,128)} %bitcast.7), custom_call_target="tpu_custom_call" | custom-call | tf_op jit(solution)/shard_map/pallas_call | solution.py:420
  32.8 1.7 %copy.8 = bf16[8,64,192]{2,1,0:T(8,128)(2,1)} copy(bf16[8,64,192]{2,1,0:T(8,128)(2,1)} %shard_map.64) | data formatting | bytes 393216

commit v5 on v4

--- a/solution.py
+++ b/solution.py
@@ -18,9 +18,9 @@
 
 
 def kernel(a_hbm, cols_hbm, p_hbm, pattern_hbm, aggregate_hbm, owners_hbm, out,
-           cols, pattern, aggregate, owners, a_v, p_v, pooled, applied, sums, packed, rim,
+           cols, pattern, aggregate, owners, a_v, p_v, pooled, applied, sums, packed, packed_side, rim, rim_side,
            edge_out, edge_in, piece_out, spread, mail_out, mail_in, table_v, table,
-           a_sem, p_sem, index_sem, rim_send, rim_recv, edge_send, edge_recv,
+           a_sem, p_sem, index_sem, rim_send, rim_recv, spill_send, spill_recv, edge_send, edge_recv,
            piece_send, piece_recv, mail_send, mail_recv, vouch):
     rows, nodes = a_hbm.shape[0], a_hbm.shape[1]
     me = lax.axis_index(AXES)
@@ -39,9 +39,9 @@
         return team * TEAM + lax.rem(seat + d, TEAM)
 
     def partner(r):
-        step = 1 << r
-        up = lax.rem(team // step, 2) == 0
-        return place_of(jnp.where(up, team + step, team - step) * TEAM + seat)
+        step = TEAM << r
+        up = lax.rem(me // step, 2) == 0
+        return place_of(jnp.where(up, me + step, me - step))
 
     after = place_of(jnp.minimum(me + 1, count - 1))
     before = place_of(jnp.maximum(me - 1, 0))
@@ -55,12 +55,12 @@
     def _():
         pl.semaphore_signal(barrier, inc=1, device_id=before, device_id_type=MESH)
 
-    for r in range(rounds):
-        pl.semaphore_signal(barrier, inc=1, device_id=partner(r), device_id_type=MESH)
-
     @pl.loop(1, TEAM)
     def _(d):
         pl.semaphore_signal(barrier, inc=1, device_id=place_of(mate(d)), device_id_type=MESH)
+
+    for r in range(rounds):
+        pl.semaphore_signal(barrier, inc=1, device_id=partner(r), device_id_type=MESH)
 
     step = 2 * GROUP
 
@@ -81,6 +81,8 @@
 
     a_wings = [a_copy(first, wing, inner + k) for k, first in enumerate((0, rows - wing))]
 
+    for k in range(2):
+        p_copy(k).start()
     index_copies = [
         pltpu.make_async_copy(source, landing, index_sem.at[k])
         for k, (source, landing) in enumerate(
@@ -94,8 +96,6 @@
     ]
     for copy in index_copies:
         copy.start()
-    for k in range(2):
-        p_copy(k).start()
 
     left = lax.broadcasted_iota(jnp.int32, (nodes, 128), 1) < 64
     lane = lax.broadcasted_iota(jnp.int32, (1, 128), 1) < 64
@@ -119,8 +119,73 @@
             else:
                 pooled[HR + i, :, 128:] = jnp.zeros_like(x0)
 
+    for k in range(2):
+        p_copy(k).wait()
+    for k in range(2, 4):
+        p_copy(k).start()
+    for k in range(inner):
+        a_inner(k).start()
+    for copy in a_wings:
+        copy.start()
+
+    @pl.loop(0, HR // 2, unroll=4)
+    def _(i):
+        for side, first in ((0, rows - HR), (1, 0)):
+            packed[side, i] = jnp.concatenate(
+                [p_v[first + i + k, :, 64:128] for k in (0, HR // 2)], axis=1
+            )
+
+    near = TEAM - 1 + rounds + jnp.where(has_after, 1, 0) + jnp.where(has_before, 1, 0)
+    pl.semaphore_wait(barrier, near)
+
+    def both_ways(outbox, inbox, send_sem, recv_sem):
+        return [
+            pltpu.make_async_remote_copy(
+                src_ref=outbox.at[side],
+                dst_ref=inbox.at[side],
+                send_sem=send_sem.at[side],
+                recv_sem=recv_sem.at[side],
+                device_id=(after, before)[side],
+                device_id_type=MESH,
+            )
+            for side in range(2)
+        ]
+
+    sends = (has_after, has_before)
+    receives = (has_before, has_after)
+    def send(copies):
+        for side in range(2):
+            @pl.when(sends[side])
+            def _():
+                copies[side].start()
+
+    rims = both_ways(packed, rim, rim_send, rim_recv)
+    spills = both_ways(packed_side, rim_side, spill_send, spill_recv)
+    send(rims)
+
+    def vouch_for(r):
+        pl.semaphore_signal(vouch.at[r], inc=1, device_id=partner(r), device_id_type=MESH)
+
+    def pass_on(r):
+        pl.semaphore_wait(vouch.at[r - 1], 1)
+        vouch_for(r)
+
+    vouch_for(0)
     for copy in index_copies:
         copy.wait()
+
+    @pl.loop(0, 2)
+    def _(end):
+        place_group(end * (groups - 1), True)
+
+    @pl.loop(0, SPR // 2, unroll=2)
+    def _(i):
+        for side, first, at in ((0, HR + rows - SPR, 192), (1, HR, 128)):
+            packed_side[side, i] = jnp.concatenate(
+                [pooled[first + i + k, :, at : at + 64] for k in (0, SPR // 2)], axis=1
+            )
+
+    send(spills)
 
     total_agg = owners.shape[1]
     down = lax.broadcasted_iota(jnp.int32, (total_agg, total_agg), 0)
@@ -136,33 +201,6 @@
     table_copy = pltpu.make_async_copy(table_v, table, index_sem.at[4])
     table_copy.start()
 
-    for k in range(2):
-        p_copy(k).wait()
-    for k in range(2, 4):
-        p_copy(k).start()
-    for k in range(inner):
-        a_inner(k).start()
-    for copy in a_wings:
-        copy.start()
-
-    @pl.loop(0, 2)
-    def _(end):
-        place_group(end * (groups - 1), True)
-
-    @pl.loop(0, HR // 2)
-    def _(i):
-        for side, first in ((0, rows - HR), (1, 0)):
-            packed[side, i] = jnp.concatenate(
-                [p_v[first + i + k, :, 64:128] for k in (0, HR // 2)], axis=1
-            )
-
-    @pl.loop(0, SPR // 2)
-    def _(i):
-        for side, first, at in ((0, HR + rows - SPR, 192), (1, HR, 128)):
-            packed[side, HR // 2 + i] = jnp.concatenate(
-                [pooled[first + i + k, :, at : at + 64] for k in (0, SPR // 2)], axis=1
-            )
-
     @pl.loop(0, 2)
     def _(end):
         place_group(1 + end * (groups - 3), False)
@@ -173,34 +211,6 @@
         pooled[rows + HR + i] = jnp.zeros((nodes, 256), BF16)
 
     sums[...] = jnp.zeros_like(sums)
-    near = TEAM - 1 + rounds + jnp.where(has_after, 1, 0) + jnp.where(has_before, 1, 0)
-    pl.semaphore_wait(barrier, near)
-
-    def both_ways(outbox, inbox, send_sem, recv_sem):
-        return [
-            pltpu.make_async_remote_copy(
-                src_ref=outbox.at[side],
-                dst_ref=inbox.at[side],
-                send_sem=send_sem.at[side],
-                recv_sem=recv_sem.at[side],
-                device_id=(after, before)[side],
-                device_id_type=MESH,
-            )
-            for side in range(2)
-        ]
-
-    sends = (has_after, has_before)
-    receives = (has_before, has_after)
-    rims = both_ways(packed, rim, rim_send, rim_recv)
-    for side in range(2):
-        @pl.when(sends[side])
-        def _():
-            rims[side].start()
-
-    def vouch_for(r):
-        pl.semaphore_signal(vouch.at[r], inc=1, device_id=partner(r), device_id_type=MESH)
-
-    vouch_for(0)
     for k in range(2, 4):
         p_copy(k).wait()
 
@@ -238,20 +248,16 @@
         first = wing + k * step
         run_pair(first, first + GROUP, GROUP, 128, 128)
 
-    pl.semaphore_wait(vouch.at[0], 1)
-    for r in range(1, rounds):
-        vouch_for(r)
-        if r < rounds - 1:
-            pl.semaphore_wait(vouch.at[r], 1)
     for copy in a_wings:
         copy.wait()
-    run_pair(HR, rows - HR - GROUP, GROUP, 128, 256)
+    pass_on(1)
 
     zero = jnp.zeros((nodes, 128), BF16)
     for side, first in enumerate((0, rows + HR)):
         @pl.when(receives[side])
         def _():
             rims[side].wait_recv()
+            spills[side].wait_recv()
             keep = left if side == 0 else ~left
 
             @pl.loop(0, HR // 2, unroll=4)
@@ -266,7 +272,7 @@
 
             @pl.loop(0, SPR // 2, unroll=2)
             def _(i):
-                both = rim[side, HR // 2 + i]
+                both = rim_side[side, i]
                 swapped = jnp.concatenate([both[:, 64:], both[:, :64]], axis=1)
                 early, late = (swapped, both) if side == 0 else (both, swapped)
                 for k, own in ((0, early), (SPR // 2, late)):
@@ -279,20 +285,15 @@
     edge_out[1, :, :64] = sums[128:192, 128:192]
     edge_out[1, :, 64:] = sums[128:192, 64:128]
     edges = both_ways(edge_out, edge_in, edge_send, edge_recv)
-    for side in range(2):
-        @pl.when(sends[side])
-        def _():
-            edges[side].start()
-
-    @pl.loop(0, 2)
-    def _(side):
-        first = SPR + side * (rows - HR - SPR)
-        apply_rows(first, HR - SPR, 0, 256)
-        add_up(first, HR - SPR, 0, 128, 256)
+    send(edges)
+
+    total = HR + GROUP - SPR
+    run_pair(SPR, rows - HR - GROUP, total, 128, 256)
 
     table_copy.wait()
-    if rounds:
-        pl.semaphore_wait(vouch.at[rounds - 1], 1)
+    for r in range(2, rounds):
+        pass_on(r)
+    pl.semaphore_wait(vouch.at[rounds - 1], 1)
     for side in range(2):
         @pl.when(receives[side])
         def _():
@@ -367,7 +368,7 @@
             device_id_type=MESH,
         )
 
-    @pl.loop(1, TEAM)
+    @pl.loop(1, TEAM, unroll=7)
     def _(d):
         fill(lax.rem(seat + d, TEAM), mail_out.at[d])
         mail_copy(d).start()
@@ -400,6 +401,7 @@
         @pl.when(sends[side])
         def _():
             rims[side].wait_send()
+            spills[side].wait_send()
             edges[side].wait_send()
 
     all_pieces.wait_send()
@@ -430,10 +432,12 @@
             pltpu.VMEM(a_blocks.shape, BF16),
             pltpu.VMEM(p_blocks.shape, BF16),
             pltpu.VMEM(pool, BF16),
-            pltpu.VMEM((2, (HR - SPR) * nodes, 4 * nodes), BF16),
+            pltpu.VMEM((2, (HR + GROUP - SPR) * nodes, 4 * nodes), BF16),
             pltpu.VMEM((4 * nodes, 4 * nodes), F32),
-            pltpu.VMEM((2, (HR + SPR) // 2, nodes, 2 * nodes), BF16),
-            pltpu.VMEM((2, (HR + SPR) // 2, nodes, 2 * nodes), BF16),
+            pltpu.VMEM((2, HR // 2, nodes, 2 * nodes), BF16),
+            pltpu.VMEM((2, SPR // 2, nodes, 2 * nodes), BF16),
+            pltpu.VMEM((2, HR // 2, nodes, 2 * nodes), BF16),
+            pltpu.VMEM((2, SPR // 2, nodes, 2 * nodes), BF16),
             pltpu.VMEM((2, nodes, 2 * nodes), F32),
             pltpu.VMEM((2, nodes, 2 * nodes), F32),
             pltpu.VMEM((TEAM, 3 * lines, 128), BF16),
@@ -449,11 +453,13 @@
             dma((2,)),
             dma((2,)),
             dma((2,)),
+            dma((2,)),
+            dma((2,)),
             dma,
             dma,
             dma,
             dma,
-            pltpu.SemaphoreType.REGULAR((max(count // TEAM - 1, 1).bit_length(),)),
+            pltpu.SemaphoreType.REGULAR((count.bit_length() - TEAM.bit_length(),)),
         ],
         compiler_params=pltpu.CompilerParams(
             collective_id=0, has_side_effects=True, vmem_limit_bytes=56 << 20

time: 34.6 us -> 33.7 us (0.974)
  Pallas kernels: 32.8 us -> 31.8 us
    pallas_call x1, Pallas kernels: 32.8 us -> 31.8 us  [shards(): pl.pallas_call(kernel, out_shape=jax.ShapeDtypeStruct((OWNMAX, nodes, 3 *...]
where the time goes in v5:
time: 33.7 us; the launch traced here: 33.5 us
  Pallas kernels  31.8 us (94%)
  local copies, waits for them, and re-layouts  1.67 us (5%)
    pallas_call x1, Pallas kernels, shards(): pl.pallas_call(kernel, out_shape=jax.ShapeDtypeStruct((OWNMAX, nodes, 3 *...  31.8 us
    unnamed x1, local copies, waits for them, and re-layouts  1.67 us

profile of v5, /device:TPU:0, one launch (start us, length us, event | category | flops | bytes accessed | tf_op | source)
XLA Modules:
  0.0 33.5 jit_solution(10402029258215653311)
XLA Ops:
  0.0 31.8 %shard_map.64 = bf16[8,64,192]{2,1,0:T(8,128)(2,1)} custom-call(bf16[192,64,512]{2,1,0:T(8,128)(2,1)} %a_hbm.1, s32[8,192]{1,0:T(8,128)} %bitcast.4, bf16[192,64,192]{2,1,0:T(8,128)(2,1)} %p_hbm.1, s32[3,192]{1,0:T(4,128)} %bitcast.5, s32[1,192]{1,0:T(1,128)} %bitcast.6, s32[1,64]{1,0:T(1,128)} %bitcast.7), custom_call_target="tpu_custom_call" | custom-call | tf_op jit(solution)/shard_map/pallas_call | solution.py:422
  31.8 1.7 %copy.8 = bf16[8,64,192]{2,1,0:T(8,128)(2,1)} copy(bf16[8,64,192]{2,1,0:T(8,128)(2,1)} %shard_map.64) | data formatting | bytes 393216

commit v6 on v5

--- a/solution.py
+++ b/solution.py
@@ -214,7 +214,7 @@
     for k in range(2, 4):
         p_copy(k).wait()
 
-    @pl.loop(2, groups - 2)
+    @pl.loop(2, groups - 2, unroll=2)
     def _(g):
         place_group(g, False)
 
@@ -242,7 +242,7 @@
         add_up(first, total, 0, high, width)
         add_up(later, total, 1, high, width)
 
-    @pl.loop(0, inner)
+    @pl.loop(0, inner, unroll=inner)
     def _(k):
         a_inner(k).wait()
         first = wing + k * step

time: 33.7 us -> 33.2 us (0.985)
  Pallas kernels: 31.8 us -> 31.3 us
    pallas_call x1, Pallas kernels: 31.8 us -> 31.3 us  [shards(): pl.pallas_call(kernel, out_shape=jax.ShapeDtypeStruct((OWNMAX, nodes, 3 *...]
where the time goes in v6:
time: 33.2 us; the launch traced here: 33 us
  Pallas kernels  31.3 us (94%)
  local copies, waits for them, and re-layouts  1.67 us (5%)
    pallas_call x1, Pallas kernels, shards(): pl.pallas_call(kernel, out_shape=jax.ShapeDtypeStruct((OWNMAX, nodes, 3 *...  31.3 us
    unnamed x1, local copies, waits for them, and re-layouts  1.67 us

profile of v6, /device:TPU:0, one launch (start us, length us, event | category | flops | bytes accessed | tf_op | source)
XLA Modules:
  0.0 33.0 jit_solution(809932397174291754)
XLA Ops:
  0.0 31.3 %shard_map.64 = bf16[8,64,192]{2,1,0:T(8,128)(2,1)} custom-call(bf16[192,64,512]{2,1,0:T(8,128)(2,1)} %a_hbm.1, s32[8,192]{1,0:T(8,128)} %bitcast.4, bf16[192,64,192]{2,1,0:T(8,128)(2,1)} %p_hbm.1, s32[3,192]{1,0:T(4,128)} %bitcast.5, s32[1,192]{1,0:T(1,128)} %bitcast.6, s32[1,64]{1,0:T(1,128)} %bitcast.7), custom_call_target="tpu_custom_call" | custom-call | tf_op jit(solution)/shard_map/pallas_call | solution.py:422
  31.4 1.7 %copy.8 = bf16[8,64,192]{2,1,0:T(8,128)(2,1)} copy(bf16[8,64,192]{2,1,0:T(8,128)(2,1)} %shard_map.64) | data formatting | bytes 393216

commit v7 on v6

--- a/solution.py
+++ b/solution.py
@@ -205,7 +205,7 @@
     def _(end):
         place_group(1 + end * (groups - 3), False)
 
-    @pl.loop(0, HR)
+    @pl.loop(0, HR, unroll=4)
     def _(i):
         pooled[i] = jnp.zeros((nodes, 256), BF16)
         pooled[rows + HR + i] = jnp.zeros((nodes, 256), BF16)

time: 33.2 us -> 33.2 us (level)
  no operation moved by 1% of the time
where the time goes in v7:
time: 33.2 us; the launch traced here: 33 us
  Pallas kernels  31.3 us (94%)
  local copies, waits for them, and re-layouts  1.67 us (5%)
    pallas_call x1, Pallas kernels, shards(): pl.pallas_call(kernel, out_shape=jax.ShapeDtypeStruct((OWNMAX, nodes, 3 *...  31.3 us
    unnamed x1, local copies, waits for them, and re-layouts  1.67 us

profile of v7, /device:TPU:0, one launch (start us, length us, event | category | flops | bytes accessed | tf_op | source)
XLA Modules:
  0.0 33.0 jit_solution(2934044946290860295)
XLA Ops:
  0.0 31.3 %shard_map.64 = bf16[8,64,192]{2,1,0:T(8,128)(2,1)} custom-call(bf16[192,64,512]{2,1,0:T(8,128)(2,1)} %a_hbm.1, s32[8,192]{1,0:T(8,128)} %bitcast.4, bf16[192,64,192]{2,1,0:T(8,128)(2,1)} %p_hbm.1, s32[3,192]{1,0:T(4,128)} %bitcast.5, s32[1,192]{1,0:T(1,128)} %bitcast.6, s32[1,64]{1,0:T(1,128)} %bitcast.7), custom_call_target="tpu_custom_call" | custom-call | tf_op jit(solution)/shard_map/pallas_call | solution.py:422
  31.4 1.7 %copy.8 = bf16[8,64,192]{2,1,0:T(8,128)(2,1)} copy(bf16[8,64,192]{2,1,0:T(8,128)(2,1)} %shard_map.64) | data formatting | bytes 393216
